TPU v7x, 512 devices: a whole 4x8x8 slice. The times are simulated.
512 devices in a mesh: ta: 128 (over y_hi, x, z), gz: 4 (over y_lo, core).
Axes of the slice: x: 4, y: 8 (y_hi: 4, y_lo: 2; y = y_hi * 2 + y_lo), z: 8, core: 2. Of those that a mesh axis runs over, the one named last changes fastest.
Arguments:
- source: bfloat16 [128, 8, 4, 4, 64, 128], P('ta', 'gz'), may hold values from -6 to 6
- self_codes: bfloat16 [128, 8, 4, 4, 64, 64], P('ta', 'gz'), may hold values from -6 to 6
- hop_codes: bfloat16 [128, 8, 4, 4, 64, 256], P('ta', 'gz'), may hold values from -6 to 6
- link_scales: bfloat16 [128, 8, 4, 4, 5], P('ta', 'gz'), may hold values from 0.019897461 to 0.079589844
- restrict_map: int32 [128, 8, 4, 4], P('ta', 'gz'), may hold values from 0 to 15
- restrictor: bfloat16 [128, 8, 4, 4, 64, 64], P('ta', 'gz'), may hold values from -0.75 to 0.75
Outputs:
- smoothed: bfloat16 [128, 8, 4, 4, 64, 128], P('ta', 'gz')
- coarse: float32 [128, 16, 64, 128], P('ta', 'gz')
All inputs are finite; a program needn't handle non-finite values.
Results may differ from a plain program's by a relative error of at most 0.0041.
Values may be sent and summed in bfloat16 or wider, within the bound.
No kernel may reach another device: no remote copies, remote signals or barrier semaphores. Data moves between devices by JAX's collectives and lax.ppermute only.
A program may use at most 64 MiB of HBM per device.

v0:
```python
import jax
import jax.numpy as jnp
from jax import lax
from jax.sharding import PartitionSpec as P

ITERS = 3
AGG_DEV = 4
OMEGA = 0.5


def shifted(block, axis, distance):
    devices = range(lax.axis_size(axis))
    route = [((i - distance) % len(devices), i) for i in devices]
    return lax.ppermute(block, axis, route)


def local_mult(codes, vector):
    return jnp.einsum("tzxyab,tzxybr->tzxyar", codes, vector, preferred_element_type=jnp.float32)


def local_mult_transposed(codes, vector):
    return jnp.einsum("tzxyab,tzxyar->tzxybr", codes, vector, preferred_element_type=jnp.float32)


def shards(source, self_codes, hop_codes, link_scales, restrict_map, restrictor):
    degrees = source.shape[4]
    blocks = [
        hop_codes[..., direction * degrees : (direction + 1) * degrees] for direction in range(4)
    ]
    scales = link_scales.astype(jnp.float32)
    factors = [scales[..., direction][..., None, None] for direction in range(5)]
    source_float = source.astype(jnp.float32)
    estimate = source_float
    vector_field = source
    for iteration in range(ITERS):
        result = vector_field.astype(jnp.float32) + factors[0] * local_mult(
            self_codes, vector_field
        )
        arrived = shifted(vector_field, "ta", -1)
        t_next = jnp.concatenate([vector_field[1:], arrived], axis=0)
        z_arrived = shifted(vector_field[:, :1], "gz", -1)
        z_next = jnp.concatenate([vector_field[:, 1:], z_arrived], axis=1)
        neighbours = [jnp.roll(vector_field, -1, 2), jnp.roll(vector_field, -1, 3), z_next, t_next]
        for operate_direction in range(4):
            result = result + factors[operate_direction + 1] * local_mult(
                blocks[operate_direction], neighbours[operate_direction]
            )
        for operate_direction in range(2):
            behind_term = (
                factors[operate_direction + 1]
                * local_mult_transposed(blocks[operate_direction], vector_field)
            ).astype(jnp.bfloat16)
            result = result + jnp.roll(behind_term, 1, axis=2 + operate_direction).astype(
                jnp.float32
            )
        z_terms = (factors[3] * local_mult_transposed(blocks[2], vector_field)).astype(jnp.bfloat16)
        z_from = shifted(z_terms[:, -1:], "gz", 1)
        result = result + jnp.concatenate([z_from, z_terms[:, :-1]], axis=1).astype(jnp.float32)
        t_terms = (factors[4] * local_mult_transposed(blocks[3], vector_field)).astype(jnp.bfloat16)
        t_from = shifted(t_terms, "ta", 1)
        t_incoming = jnp.concatenate([t_from, t_terms[:-1]], axis=0)
        applied = result + t_incoming.astype(jnp.float32)
        estimate = estimate + OMEGA * (source_float - applied)
        vector_field = estimate.astype(jnp.bfloat16)
    coarse_width = restrictor.shape[4]
    right_cols = source.shape[5]
    site_count = source.shape[0] * source.shape[1] * source.shape[2] * source.shape[3]
    projected = jnp.einsum(
        "tzxyca,tzxyar->tzxycr", restrictor, vector_field, preferred_element_type=jnp.float32
    )
    flattened = projected.reshape(site_count, coarse_width * right_cols)
    groups = AGG_DEV * lax.axis_size("gz")
    labels = restrict_map.reshape(site_count)
    onehot = (labels[None, :] == jnp.arange(groups, dtype=jnp.int32)[:, None]).astype(jnp.float32)
    partial_sums = jnp.dot(onehot, flattened, precision=lax.Precision.HIGHEST)
    summed = lax.psum(partial_sums, "gz")
    owned = lax.dynamic_slice_in_dim(summed, lax.axis_index("gz") * AGG_DEV, AGG_DEV, 0)
    return (vector_field, owned.reshape(1, AGG_DEV, coarse_width, right_cols))


def solution(mesh):
    placed = (
        P("ta", "gz", None, None, None, None),
        P("ta", "gz", None, None, None, None),
        P("ta", "gz", None, None, None, None),
        P("ta", "gz", None, None, None),
        P("ta", "gz", None, None),
        P("ta", "gz", None, None, None, None),
    )
    return jax.shard_map(
        shards,
        mesh=mesh,
        in_specs=placed,
        out_specs=(P("ta", "gz", None, None, None, None), P("ta", "gz", None, None)),
        check_vma=False,
    )
```

profile of v0, /device:TPU:1, one launch (start us, length us, event | category | flops | bytes accessed | tf_op | source)
XLA Modules:
  0.0 201.6 jit_solution(1051310907819398375)
XLA Ops:
  7.2 17.5 %collective-permute-start.1 = (bf16[1,2,4,4,64,128]{5,4,3,2,1,0:T(8,128)(2,1)}, bf16[1,2,4,4,64,128]{5,4,3,2,1,0:T(8,128)(2,1)}, u32[]{:S(2)}, u32[]{:S(2)}) collective-permute-start(bf16[1,2,4,4,64,128]{5,4,3,2,1,0:T(8,128)(2,1)} %param.6), channel_id=1, source_target_pairs={{4,0},{8,4},{12,8},{16,12},{20,16},{24,20},{28,24},{32,28},{36,32}... | collective-permute-start | bytes 1572872 | tf_op jit(solution)/shard_map/ppermute | solution.py:14
  25.7 1.6 fusion.66
  27.4 0.8 fusion.176
  28.1 3.1 %collective-permute-start.2 = (bf16[1,1,4,4,64,128]{5,4,3,2,1,0:T(8,128)(2,1)}, bf16[1,1,4,4,64,128]{5,4,3,2,1,0:T(8,128)(2,1)}, u32[]{:S(2)}, u32[]{:S(2)}) collective-permute-start(bf16[1,1,4,4,64,128]{5,4,3,2,1,0:T(8,128)(2,1)} %get-tuple-element.15), channel_id=1, source_target_pairs={{3,0},{0,1},{1,2},{2,3},{7,4},{4,5},{5,6},{6,7},{11,8},{8,9},{9,10... | collective-permute-start | bytes 786440 | tf_op jit(solution)/shard_map/ppermute | solution.py:14
  31.3 1.4 fusion.65
  32.7 1.9 collective-permute-start.3
  34.6 0.9 fusion.177
  35.5 1.9 collective-permute-start
  40.2 0.8 copy-done.6
  41.8 5.1 %collective-permute-done.1 = bf16[1,2,4,4,64,128]{5,4,3,2,1,0:T(8,128)(2,1)} collective-permute-done((bf16[1,2,4,4,64,128]{5,4,3,2,1,0:T(8,128)(2,1)}, bf16[1,2,4,4,64,128]{5,4,3,2,1,0:T(8,128)(2,1)}, u32[]{:S(2)}, u32[]{:S(2)}) %collective-permute-start.1) | collective-permute-done | bytes 524320 | tf_op jit(solution)/shard_map/ppermute | solution.py:14
  46.9 1.4 fusion.13
  48.3 5.4 %collective-permute-done = bf16[1,1,4,4,64,128]{5,4,3,2,1,0:T(8,128)(2,1)} collective-permute-done((bf16[1,1,4,4,64,128]{5,4,3,2,1,0:T(8,128)(2,1)}, bf16[1,1,4,4,64,128]{5,4,3,2,1,0:T(8,128)(2,1)}, u32[]{:S(2)}, u32[]{:S(2)}) %collective-permute-start) | collective-permute-done | bytes 262176 | tf_op jit(solution)/shard_map/ppermute | solution.py:14
  53.7 12.5 %collective-permute-done.3 = bf16[1,2,4,4,64,128]{5,4,3,2,1,0:T(8,128)(2,1)} collective-permute-done((bf16[1,2,4,4,64,128]{5,4,3,2,1,0:T(8,128)(2,1)}, bf16[1,2,4,4,64,128]{5,4,3,2,1,0:T(8,128)(2,1)}, u32[]{:S(2)}, u32[]{:S(2)}) %collective-permute-start.3) | collective-permute-done | bytes 524320 | tf_op jit(solution)/shard_map/ppermute | solution.py:14
  66.2 1.9 fusion.178
  68.2 1.9 collective-permute-start.5
  71.5 0.8 copy-done.7
  72.4 2.1 %collective-permute-start.6 = (bf16[1,1,4,4,64,128]{5,4,3,2,1,0:T(8,128)(2,1)S(1)}, bf16[1,1,4,4,64,128]{5,4,3,2,1,0:T(8,128)(2,1)S(1)}, u32[]{:S(2)}, u32[]{:S(2)}) collective-permute-start(bf16[1,1,4,4,64,128]{5,4,3,2,1,0:T(8,128)(2,1)S(1)} %get-tuple-element.11), channel_id=1, source_target_pairs={{3,0},{0,1},{1,2},{2,3},{7,4},{4,5},{5,6},{6,7},{11,8},{8,9},{9,10... | collective-permute-start | bytes 786440 | tf_op jit(solution)/shard_map/ppermute | solution.py:14
  74.5 3.6 %collective-permute-start.7 = (bf16[1,2,4,4,64,128]{5,4,3,2,1,0:T(8,128)(2,1)S(1)}, bf16[1,2,4,4,64,128]{5,4,3,2,1,0:T(8,128)(2,1)S(1)}, u32[]{:S(2)}, u32[]{:S(2)}) collective-permute-start(bf16[1,2,4,4,64,128]{5,4,3,2,1,0:T(8,128)(2,1)S(1)} %fusion.61), channel_id=1, source_target_pairs={{508,0},{0,4},{4,8},{8,12},{12,16},{16,20},{20,24},{24,28},{28,32}... | collective-permute-start | bytes 1572872 | tf_op jit(solution)/shard_map/ppermute | solution.py:14
  78.1 2.8 %collective-permute-start.4 = (bf16[1,1,4,4,64,128]{5,4,3,2,1,0:T(8,128)(2,1)S(1)}, bf16[1,1,4,4,64,128]{5,4,3,2,1,0:T(8,128)(2,1)S(1)}, u32[]{:S(2)}, u32[]{:S(2)}) collective-permute-start(bf16[1,1,4,4,64,128]{5,4,3,2,1,0:T(8,128)(2,1)S(1)} %get-tuple-element.14), channel_id=1, source_target_pairs={{1,0},{2,1},{3,2},{0,3},{5,4},{6,5},{7,6},{4,7},{9,8},{10,9},{11,1... | collective-permute-start | bytes 786440 | tf_op jit(solution)/shard_map/ppermute | solution.py:14
  82.7 0.8 copy-done.8
  83.5 9.1 %collective-permute-done.5 = bf16[1,2,4,4,64,128]{5,4,3,2,1,0:T(8,128)(2,1)S(1)} collective-permute-done((bf16[1,2,4,4,64,128]{5,4,3,2,1,0:T(8,128)(2,1)S(1)}, bf16[1,2,4,4,64,128]{5,4,3,2,1,0:T(8,128)(2,1)S(1)}, u32[]{:S(2)}, u32[]{:S(2)}) %collective-permute-start.5) | collective-permute-done | bytes 524320 | tf_op jit(solution)/shard_map/ppermute | solution.py:14
  93.0 10.9 %collective-permute-done.7 = bf16[1,2,4,4,64,128]{5,4,3,2,1,0:T(8,128)(2,1)S(1)} collective-permute-done((bf16[1,2,4,4,64,128]{5,4,3,2,1,0:T(8,128)(2,1)S(1)}, bf16[1,2,4,4,64,128]{5,4,3,2,1,0:T(8,128)(2,1)S(1)}, u32[]{:S(2)}, u32[]{:S(2)}) %collective-permute-start.7) | collective-permute-done | bytes 524320 | tf_op jit(solution)/shard_map/ppermute | solution.py:14
  104.7 1.9 collective-permute-start.9
  108.9 7.5 %collective-permute-start.10 = (bf16[1,1,4,4,64,128]{5,4,3,2,1,0:T(8,128)(2,1)S(1)}, bf16[1,1,4,4,64,128]{5,4,3,2,1,0:T(8,128)(2,1)S(1)}, u32[]{:S(2)}, u32[]{:S(2)}) collective-permute-start(bf16[1,1,4,4,64,128]{5,4,3,2,1,0:T(8,128)(2,1)S(1)} %get-tuple-element.7), channel_id=1, source_target_pairs={{3,0},{0,1},{1,2},{2,3},{7,4},{4,5},{5,6},{6,7},{11,8},{8,9},{9,10... | collective-permute-start | bytes 786440 | tf_op jit(solution)/shard_map/ppermute | solution.py:14
  116.4 3.6 %collective-permute-start.11 = (bf16[1,2,4,4,64,128]{5,4,3,2,1,0:T(8,128)(2,1)S(1)}, bf16[1,2,4,4,64,128]{5,4,3,2,1,0:T(8,128)(2,1)S(1)}, u32[]{:S(2)}, u32[]{:S(2)}) collective-permute-start(bf16[1,2,4,4,64,128]{5,4,3,2,1,0:T(8,128)(2,1)S(1)} %fusion.57), channel_id=1, source_target_pairs={{508,0},{0,4},{4,8},{8,12},{12,16},{16,20},{20,24},{24,28},{28,32}... | collective-permute-start | bytes 1572872 | tf_op jit(solution)/shard_map/ppermute | solution.py:14
  120.0 2.1 %collective-permute-start.8 = (bf16[1,1,4,4,64,128]{5,4,3,2,1,0:T(8,128)(2,1)S(1)}, bf16[1,1,4,4,64,128]{5,4,3,2,1,0:T(8,128)(2,1)S(1)}, u32[]{:S(2)}, u32[]{:S(2)}) collective-permute-start(bf16[1,1,4,4,64,128]{5,4,3,2,1,0:T(8,128)(2,1)S(1)} %get-tuple-element.10), channel_id=1, source_target_pairs={{1,0},{2,1},{3,2},{0,3},{5,4},{6,5},{7,6},{4,7},{9,8},{10,9},{11,1... | collective-permute-start | bytes 786440 | tf_op jit(solution)/shard_map/ppermute | solution.py:14
  123.9 0.8 copy-done.5
  125.0 11.4 %collective-permute-done.8 = bf16[1,1,4,4,64,128]{5,4,3,2,1,0:T(8,128)(2,1)S(1)} collective-permute-done((bf16[1,1,4,4,64,128]{5,4,3,2,1,0:T(8,128)(2,1)S(1)}, bf16[1,1,4,4,64,128]{5,4,3,2,1,0:T(8,128)(2,1)S(1)}, u32[]{:S(2)}, u32[]{:S(2)}) %collective-permute-start.8) | collective-permute-done | bytes 262176 | tf_op jit(solution)/shard_map/ppermute | solution.py:14
  136.5 11.5 %collective-permute-done.11 = bf16[1,2,4,4,64,128]{5,4,3,2,1,0:T(8,128)(2,1)S(1)} collective-permute-done((bf16[1,2,4,4,64,128]{5,4,3,2,1,0:T(8,128)(2,1)S(1)}, bf16[1,2,4,4,64,128]{5,4,3,2,1,0:T(8,128)(2,1)S(1)}, u32[]{:S(2)}, u32[]{:S(2)}) %collective-permute-start.11) | collective-permute-done | bytes 524320 | tf_op jit(solution)/shard_map/ppermute | solution.py:14
  149.9 1.9 fusion.69
  151.8 41.3 %all-reduce.2.cloned.1.call-done = f32[16,8192]{1,0:T(8,128)} async-done(((f32[16,8192]{1,0:T(8,128)}), f32[16,8192]{1,0:T(8,128)}) %all-reduce.2.cloned.1.call-update) | async-done | bytes 524304 | tf_op jit(solution)/shard_map/psum | solution.py:76
  193.2 1.0 dynamic-slice_bitcast_fusion
  (97 shorter events, 15.5 us)
Async XLA Ops:
  7.2 30.3 %copy-start = (bf16[1,2,4,4,64,64]{5,4,3,2,1,0:T(8,128)(2,1)S(1)}, bf16[1,2,4,4,64,64]{5,4,3,2,1,0:T(8,128)(2,1)}, u32[]{:S(2)}) copy-start(bf16[1,2,4,4,64,64]{5,4,3,2,1,0:T(8,128)(2,1)} %param.7) | copy-start | bytes 786436
  7.2 186.0 %all-reduce.2.cloned.1.call-start = ((), (), s32[]{:S(2)}) async-start(), calls=%async_computation | async-start | bytes 1048576 | tf_op jit(solution)/shard_map/psum | solution.py:76
  7.2 39.7 %collective-permute-start.1 = (bf16[1,2,4,4,64,128]{5,4,3,2,1,0:T(8,128)(2,1)}, bf16[1,2,4,4,64,128]{5,4,3,2,1,0:T(8,128)(2,1)}, u32[]{:S(2)}, u32[]{:S(2)}) collective-permute-start(bf16[1,2,4,4,64,128]{5,4,3,2,1,0:T(8,128)(2,1)} %param.6), channel_id=1, source_target_pairs={{4,0},{8,4},{12,8},{16,12},{20,16},{24,20},{28,24},{32,28},{36,32}... | collective-permute-start | bytes 1572872 | tf_op jit(solution)/shard_map/ppermute | solution.py:14
  25.7 5.6 %copy-start.1 = (bf16[1,2,4,4,64,256]{5,4,3,2,1,0:T(8,128)(2,1)S(1)}, bf16[1,2,4,4,64,256]{5,4,3,2,1,0:T(8,128)(2,1)}, u32[]{:S(2)}) copy-start(bf16[1,2,4,4,64,256]{5,4,3,2,1,0:T(8,128)(2,1)} %param.8) | copy-start | bytes 3145732
  27.3 3.9 %copy-start.2 = (bf16[1,2,4,4,64,128]{5,4,3,2,1,0:T(8,128)(2,1)S(1)}, bf16[1,2,4,4,64,128]{5,4,3,2,1,0:T(8,128)(2,1)}, u32[]{:S(2)}) copy-start(bf16[1,2,4,4,64,128]{5,4,3,2,1,0:T(8,128)(2,1)} %param.6) | copy-start | bytes 1572868
  28.1 20.2 %collective-permute-start.2 = (bf16[1,1,4,4,64,128]{5,4,3,2,1,0:T(8,128)(2,1)}, bf16[1,1,4,4,64,128]{5,4,3,2,1,0:T(8,128)(2,1)}, u32[]{:S(2)}, u32[]{:S(2)}) collective-permute-start(bf16[1,1,4,4,64,128]{5,4,3,2,1,0:T(8,128)(2,1)} %get-tuple-element.15), channel_id=1, source_target_pairs={{3,0},{0,1},{1,2},{2,3},{7,4},{4,5},{5,6},{6,7},{11,8},{8,9},{9,10... | collective-permute-start | bytes 786440 | tf_op jit(solution)/shard_map/ppermute | solution.py:14
  32.7 33.5 %collective-permute-start.3 = (bf16[1,2,4,4,64,128]{5,4,3,2,1,0:T(8,128)(2,1)}, bf16[1,2,4,4,64,128]{5,4,3,2,1,0:T(8,128)(2,1)}, u32[]{:S(2)}, u32[]{:S(2)}) collective-permute-start(bf16[1,2,4,4,64,128]{5,4,3,2,1,0:T(8,128)(2,1)} %fusion.65), channel_id=1, source_target_pairs={{508,0},{0,4},{4,8},{8,12},{12,16},{16,20},{20,24},{24,28},{28,32}... | collective-permute-start | bytes 1572872 | tf_op jit(solution)/shard_map/ppermute | solution.py:14
  35.5 18.3 %collective-permute-start = (bf16[1,1,4,4,64,128]{5,4,3,2,1,0:T(8,128)(2,1)}, bf16[1,1,4,4,64,128]{5,4,3,2,1,0:T(8,128)(2,1)}, u32[]{:S(2)}, u32[]{:S(2)}) collective-permute-start(bf16[1,1,4,4,64,128]{5,4,3,2,1,0:T(8,128)(2,1)} %get-tuple-element.18), channel_id=1, source_target_pairs={{1,0},{2,1},{3,2},{0,3},{5,4},{6,5},{7,6},{4,7},{9,8},{10,9},{11,1... | collective-permute-start | bytes 786440 | tf_op jit(solution)/shard_map/ppermute | solution.py:14
  41.8 24.4 %slice-start.2 = ((bf16[1,2,4,4,64,128]{5,4,3,2,1,0:T(8,128)(2,1)}), bf16[1,2,3,4,64,128]{5,4,3,2,1,0:T(8,128)(2,1)S(1)}, s32[]{:S(2)}) async-start(bf16[1,2,4,4,64,128]{5,4,3,2,1,0:T(8,128)(2,1)} %copy-done.4), calls=%async_computation.3 | async-start | bytes 786432 | tf_op jit(solution)/shard_map/jit(_roll_static)/slice | solution.py:53
  41.8 24.4 %slice-start.3 = ((bf16[1,2,4,4,64,128]{5,4,3,2,1,0:T(8,128)(2,1)}), bf16[1,2,1,4,64,128]{5,4,3,2,1,0:T(8,128)(2,1)S(1)}, s32[]{:S(2)}) async-start(bf16[1,2,4,4,64,128]{5,4,3,2,1,0:T(8,128)(2,1)} %copy-done.4), calls=%async_computation.4 | async-start | bytes 262144 | tf_op jit(solution)/shard_map/jit(_roll_static)/slice | solution.py:53
  41.8 24.4 %slice-start.6 = ((bf16[1,2,4,4,64,128]{5,4,3,2,1,0:T(8,128)(2,1)}), bf16[1,2,4,3,64,128]{5,4,3,2,1,0:T(8,128)(2,1)S(1)}, s32[]{:S(2)}) async-start(bf16[1,2,4,4,64,128]{5,4,3,2,1,0:T(8,128)(2,1)} %copy-done.6), calls=%async_computation.7 | async-start | bytes 786432 | tf_op jit(solution)/shard_map/jit(_roll_static)/slice | solution.py:53
  41.8 24.4 %slice-start.7 = ((bf16[1,2,4,4,64,128]{5,4,3,2,1,0:T(8,128)(2,1)}), bf16[1,2,4,1,64,128]{5,4,3,2,1,0:T(8,128)(2,1)S(1)}, s32[]{:S(2)}) async-start(bf16[1,2,4,4,64,128]{5,4,3,2,1,0:T(8,128)(2,1)} %copy-done.6), calls=%async_computation.8 | async-start | bytes 262144 | tf_op jit(solution)/shard_map/jit(_roll_static)/slice | solution.py:53
  41.8 24.4 %copy-start.10 = (bf16[1,1,4,4,64,128]{5,4,3,2,1,0:T(8,128)(2,1)S(1)}, bf16[1,1,4,4,64,128]{5,4,3,2,1,0:T(8,128)(2,1)}, u32[]{:S(2)}) copy-start(bf16[1,1,4,4,64,128]{5,4,3,2,1,0:T(8,128)(2,1)} %get-tuple-element.17) | copy-start | bytes 786436
  68.2 24.4 %collective-permute-start.5 = (bf16[1,2,4,4,64,128]{5,4,3,2,1,0:T(8,128)(2,1)S(1)}, bf16[1,2,4,4,64,128]{5,4,3,2,1,0:T(8,128)(2,1)S(1)}, u32[]{:S(2)}, u32[]{:S(2)}) collective-permute-start(bf16[1,2,4,4,64,128]{5,4,3,2,1,0:T(8,128)(2,1)S(1)} %get-tuple-element.19), channel_id=1, source_target_pairs={{4,0},{8,4},{12,8},{16,12},{20,16},{24,20},{28,24},{32,28},{36,32}... | collective-permute-start | bytes 1572872 | tf_op jit(solution)/shard_map/ppermute | solution.py:14
  72.4 20.5 %collective-permute-start.6 = (bf16[1,1,4,4,64,128]{5,4,3,2,1,0:T(8,128)(2,1)S(1)}, bf16[1,1,4,4,64,128]{5,4,3,2,1,0:T(8,128)(2,1)S(1)}, u32[]{:S(2)}, u32[]{:S(2)}) collective-permute-start(bf16[1,1,4,4,64,128]{5,4,3,2,1,0:T(8,128)(2,1)S(1)} %get-tuple-element.11), channel_id=1, source_target_pairs={{3,0},{0,1},{1,2},{2,3},{7,4},{4,5},{5,6},{6,7},{11,8},{8,9},{9,10... | collective-permute-start | bytes 786440 | tf_op jit(solution)/shard_map/ppermute | solution.py:14
  74.5 29.4 %collective-permute-start.7 = (bf16[1,2,4,4,64,128]{5,4,3,2,1,0:T(8,128)(2,1)S(1)}, bf16[1,2,4,4,64,128]{5,4,3,2,1,0:T(8,128)(2,1)S(1)}, u32[]{:S(2)}, u32[]{:S(2)}) collective-permute-start(bf16[1,2,4,4,64,128]{5,4,3,2,1,0:T(8,128)(2,1)S(1)} %fusion.61), channel_id=1, source_target_pairs={{508,0},{0,4},{4,8},{8,12},{12,16},{16,20},{20,24},{24,28},{28,32}... | collective-permute-start | bytes 1572872 | tf_op jit(solution)/shard_map/ppermute | solution.py:14
  78.1 14.8 %collective-permute-start.4 = (bf16[1,1,4,4,64,128]{5,4,3,2,1,0:T(8,128)(2,1)S(1)}, bf16[1,1,4,4,64,128]{5,4,3,2,1,0:T(8,128)(2,1)S(1)}, u32[]{:S(2)}, u32[]{:S(2)}) collective-permute-start(bf16[1,1,4,4,64,128]{5,4,3,2,1,0:T(8,128)(2,1)S(1)} %get-tuple-element.14), channel_id=1, source_target_pairs={{1,0},{2,1},{3,2},{0,3},{5,4},{6,5},{7,6},{4,7},{9,8},{10,9},{11,1... | collective-permute-start | bytes 786440 | tf_op jit(solution)/shard_map/ppermute | solution.py:14
  82.6 0.8 copy-start.8
  83.4 20.5 %slice-start.8 = ((bf16[1,2,4,4,64,128]{5,4,3,2,1,0:T(8,128)(2,1)}), bf16[1,2,3,4,64,128]{5,4,3,2,1,0:T(8,128)(2,1)S(1)}, s32[]{:S(2)}) async-start(bf16[1,2,4,4,64,128]{5,4,3,2,1,0:T(8,128)(2,1)} %copy-done.7), calls=%async_computation.9 | async-start | bytes 786432 | tf_op jit(solution)/shard_map/jit(_roll_static)/slice | solution.py:53
  83.4 20.5 %slice-start.9 = ((bf16[1,2,4,4,64,128]{5,4,3,2,1,0:T(8,128)(2,1)}), bf16[1,2,1,4,64,128]{5,4,3,2,1,0:T(8,128)(2,1)S(1)}, s32[]{:S(2)}) async-start(bf16[1,2,4,4,64,128]{5,4,3,2,1,0:T(8,128)(2,1)} %copy-done.7), calls=%async_computation.10 | async-start | bytes 262144 | tf_op jit(solution)/shard_map/jit(_roll_static)/slice | solution.py:53
  83.4 20.5 %slice-start.10 = ((bf16[1,2,4,4,64,128]{5,4,3,2,1,0:T(8,128)(2,1)}), bf16[1,2,4,3,64,128]{5,4,3,2,1,0:T(8,128)(2,1)S(1)}, s32[]{:S(2)}) async-start(bf16[1,2,4,4,64,128]{5,4,3,2,1,0:T(8,128)(2,1)} %copy-done.8), calls=%async_computation.11 | async-start | bytes 786432 | tf_op jit(solution)/shard_map/jit(_roll_static)/slice | solution.py:53
  83.5 20.5 %slice-start.11 = ((bf16[1,2,4,4,64,128]{5,4,3,2,1,0:T(8,128)(2,1)}), bf16[1,2,4,1,64,128]{5,4,3,2,1,0:T(8,128)(2,1)S(1)}, s32[]{:S(2)}) async-start(bf16[1,2,4,4,64,128]{5,4,3,2,1,0:T(8,128)(2,1)} %copy-done.8), calls=%async_computation.12 | async-start | bytes 262144 | tf_op jit(solution)/shard_map/jit(_roll_static)/slice | solution.py:53
  104.7 19.9 %collective-permute-start.9 = (bf16[1,2,4,4,64,128]{5,4,3,2,1,0:T(8,128)(2,1)S(1)}, bf16[1,2,4,4,64,128]{5,4,3,2,1,0:T(8,128)(2,1)S(1)}, u32[]{:S(2)}, u32[]{:S(2)}) collective-permute-start(bf16[1,2,4,4,64,128]{5,4,3,2,1,0:T(8,128)(2,1)S(1)} %get-tuple-element.21), channel_id=1, source_target_pairs={{4,0},{8,4},{12,8},{16,12},{20,16},{24,20},{28,24},{32,28},{36,32}... | collective-permute-start | bytes 1572872 | tf_op jit(solution)/shard_map/ppermute | solution.py:14
  108.0 0.8 copy-start.3
  108.9 16.2 %collective-permute-start.10 = (bf16[1,1,4,4,64,128]{5,4,3,2,1,0:T(8,128)(2,1)S(1)}, bf16[1,1,4,4,64,128]{5,4,3,2,1,0:T(8,128)(2,1)S(1)}, u32[]{:S(2)}, u32[]{:S(2)}) collective-permute-start(bf16[1,1,4,4,64,128]{5,4,3,2,1,0:T(8,128)(2,1)S(1)} %get-tuple-element.7), channel_id=1, source_target_pairs={{3,0},{0,1},{1,2},{2,3},{7,4},{4,5},{5,6},{6,7},{11,8},{8,9},{9,10... | collective-permute-start | bytes 786440 | tf_op jit(solution)/shard_map/ppermute | solution.py:14
  116.4 31.7 %collective-permute-start.11 = (bf16[1,2,4,4,64,128]{5,4,3,2,1,0:T(8,128)(2,1)S(1)}, bf16[1,2,4,4,64,128]{5,4,3,2,1,0:T(8,128)(2,1)S(1)}, u32[]{:S(2)}, u32[]{:S(2)}) collective-permute-start(bf16[1,2,4,4,64,128]{5,4,3,2,1,0:T(8,128)(2,1)S(1)} %fusion.57), channel_id=1, source_target_pairs={{508,0},{0,4},{4,8},{8,12},{12,16},{16,20},{20,24},{24,28},{28,32}... | collective-permute-start | bytes 1572872 | tf_op jit(solution)/shard_map/ppermute | solution.py:14
  120.0 16.5 %collective-permute-start.8 = (bf16[1,1,4,4,64,128]{5,4,3,2,1,0:T(8,128)(2,1)S(1)}, bf16[1,1,4,4,64,128]{5,4,3,2,1,0:T(8,128)(2,1)S(1)}, u32[]{:S(2)}, u32[]{:S(2)}) collective-permute-start(bf16[1,1,4,4,64,128]{5,4,3,2,1,0:T(8,128)(2,1)S(1)} %get-tuple-element.10), channel_id=1, source_target_pairs={{1,0},{2,1},{3,2},{0,3},{5,4},{6,5},{7,6},{4,7},{9,8},{10,9},{11,1... | collective-permute-start | bytes 786440 | tf_op jit(solution)/shard_map/ppermute | solution.py:14
  124.6 23.4 %slice-start = ((bf16[1,2,4,4,64,128]{5,4,3,2,1,0:T(8,128)(2,1)}), bf16[1,2,3,4,64,128]{5,4,3,2,1,0:T(8,128)(2,1)S(1)}, s32[]{:S(2)}) async-start(bf16[1,2,4,4,64,128]{5,4,3,2,1,0:T(8,128)(2,1)} %copy-done.3), calls=%async_computation.1 | async-start | bytes 786432 | tf_op jit(solution)/shard_map/jit(_roll_static)/slice | solution.py:53
  124.6 23.4 %slice-start.1 = ((bf16[1,2,4,4,64,128]{5,4,3,2,1,0:T(8,128)(2,1)}), bf16[1,2,1,4,64,128]{5,4,3,2,1,0:T(8,128)(2,1)S(1)}, s32[]{:S(2)}) async-start(bf16[1,2,4,4,64,128]{5,4,3,2,1,0:T(8,128)(2,1)} %copy-done.3), calls=%async_computation.2 | async-start | bytes 262144 | tf_op jit(solution)/shard_map/jit(_roll_static)/slice | solution.py:53
  124.6 23.4 %slice-start.4 = ((bf16[1,2,4,4,64,128]{5,4,3,2,1,0:T(8,128)(2,1)}), bf16[1,2,4,3,64,128]{5,4,3,2,1,0:T(8,128)(2,1)S(1)}, s32[]{:S(2)}) async-start(bf16[1,2,4,4,64,128]{5,4,3,2,1,0:T(8,128)(2,1)} %copy-done.5), calls=%async_computation.5 | async-start | bytes 786432 | tf_op jit(solution)/shard_map/jit(_roll_static)/slice | solution.py:53
  124.6 23.4 %slice-start.5 = ((bf16[1,2,4,4,64,128]{5,4,3,2,1,0:T(8,128)(2,1)}), bf16[1,2,4,1,64,128]{5,4,3,2,1,0:T(8,128)(2,1)S(1)}, s32[]{:S(2)}) async-start(bf16[1,2,4,4,64,128]{5,4,3,2,1,0:T(8,128)(2,1)} %copy-done.5), calls=%async_computation.6 | async-start | bytes 262144 | tf_op jit(solution)/shard_map/jit(_roll_static)/slice | solution.py:53
  148.1 1.0 copy-start.11
  (6 other events, 4.6 us)
Sparse Core Ops, SparseCore 0:
  151.9 41.1 all-reduce.1
where the time goes:
time: 202 us
  waiting for transfers between devices  107 us (53%)
  starting transfers between devices  50.1 us (25%)
  matrix products  18.6 us (9%)
  between operations  14.7 us (7%)
  local copies, waits for them, and re-layouts  10.1 us (5%)
    ppermute x12, waiting for transfers between devices, shifted(): return lax.ppermute(block, axis, route)  66.1 us
    ppermute x12, starting transfers between devices, shifted(): return lax.ppermute(block, axis, route)  50.1 us
    psum x1, waiting for transfers between devices, shards(): summed = lax.psum(partial_sums, 'gz')  41.3 us
    dot_general x15, matrix products, local_mult(): jnp.einsum('tzxyab,tzxybr->tzxyar', codes, vector, preferred_element_type...  8.42 us
    dot_general x12, matrix products, local_mult_transposed(): jnp.einsum('tzxyab,tzxyar->tzxybr', codes, vector, preferred_element_type...  8.03 us
    unnamed x28, local copies, waits for them, and re-layouts  7.74 us
  transfers between devices with their start and end apart: 13, of which 8 were waited for; matrix products, arithmetic and copies ran while one was open for 8% of the time, Pallas kernels for 0%

commit v1 on v0

--- a/solution.py
+++ b/solution.py
@@ -73,7 +73,8 @@
     labels = restrict_map.reshape(site_count)
     onehot = (labels[None, :] == jnp.arange(groups, dtype=jnp.int32)[:, None]).astype(jnp.float32)
     partial_sums = jnp.dot(onehot, flattened, precision=lax.Precision.HIGHEST)
-    summed = lax.psum(partial_sums, "gz")
+    parts = lax.all_gather(partial_sums, "gz")
+    summed = jnp.sum(parts, axis=0)
     owned = lax.dynamic_slice_in_dim(summed, lax.axis_index("gz") * AGG_DEV, AGG_DEV, 0)
     return (vector_field, owned.reshape(1, AGG_DEV, coarse_width, right_cols))
 

time: 202 us -> 188 us (0.931)
  waiting for transfers between devices: 107 us -> 94.6 us
  local copies, waits for them, and re-layouts: 10.1 us -> 6.71 us
    psum x1 -> x0, waiting for transfers between devices: 41.3 us -> none  [shards(): summed = lax.psum(partial_sums, 'gz')]
    all_gather x0 -> x1, waiting for transfers between devices: none -> 27.6 us  [shards(): parts = lax.all_gather(partial_sums, 'gz')]
    unnamed x28 -> x30, local copies, waits for them, and re-layouts: 7.74 us -> 2.93 us
  transfers between devices with their start and end apart: 13 -> 13, of which waited for: 8 -> 8; matrix products, arithmetic and copies ran while one was open for 8% -> 9% of each run, Pallas kernels for 0% -> 0%
where the time goes in v1:
time: 188 us; the launch traced here: 187 us
  waiting for transfers between devices  94.6 us (50%)
  starting transfers between devices  50.1 us (27%)
  matrix products  18.5 us (10%)
  between operations  14.8 us (8%)
  local copies, waits for them, and re-layouts  6.71 us (4%)
  other arithmetic  2.46 us (1%)
    ppermute x12, waiting for transfers between devices, shifted(): return lax.ppermute(block, axis, route)  67 us
    ppermute x12, starting transfers between devices, shifted(): return lax.ppermute(block, axis, route)  50.1 us
    all_gather x1, waiting for transfers between devices, shards(): parts = lax.all_gather(partial_sums, 'gz')  27.6 us
    dot_general x15, matrix products, local_mult(): jnp.einsum('tzxyab,tzxybr->tzxyar', codes, vector, preferred_element_type...  8.4 us
    dot_general x12, matrix products, local_mult_transposed(): jnp.einsum('tzxyab,tzxyar->tzxybr', codes, vector, preferred_element_type...  7.94 us
  transfers between devices with their start and end apart: 13, of which 8 were waited for; matrix products, arithmetic and copies ran while one was open for 9% of the time, Pallas kernels for 0%

profile of v1, /device:TPU:1, one launch (start us, length us, event | category | flops | bytes accessed | tf_op | source)
XLA Modules:
  0.0 187.1 jit_solution(1455762997884588242)
XLA Ops:
  7.2 17.5 %collective-permute-start.1 = (bf16[1,2,4,4,64,128]{5,4,3,2,1,0:T(8,128)(2,1)}, bf16[1,2,4,4,64,128]{5,4,3,2,1,0:T(8,128)(2,1)}, u32[]{:S(2)}, u32[]{:S(2)}) collective-permute-start(bf16[1,2,4,4,64,128]{5,4,3,2,1,0:T(8,128)(2,1)} %param.6), channel_id=1, source_target_pairs={{4,0},{8,4},{12,8},{16,12},{20,16},{24,20},{28,24},{32,28},{36,32}... | collective-permute-start | bytes 1572872 | tf_op jit(solution)/shard_map/ppermute | solution.py:14
  25.7 1.6 fusion.66
  27.3 0.8 fusion.176
  28.1 3.1 %collective-permute-start.2 = (bf16[1,1,4,4,64,128]{5,4,3,2,1,0:T(8,128)(2,1)}, bf16[1,1,4,4,64,128]{5,4,3,2,1,0:T(8,128)(2,1)}, u32[]{:S(2)}, u32[]{:S(2)}) collective-permute-start(bf16[1,1,4,4,64,128]{5,4,3,2,1,0:T(8,128)(2,1)} %get-tuple-element.15), channel_id=1, source_target_pairs={{3,0},{0,1},{1,2},{2,3},{7,4},{4,5},{5,6},{6,7},{11,8},{8,9},{9,10... | collective-permute-start | bytes 786440 | tf_op jit(solution)/shard_map/ppermute | solution.py:14
  31.3 1.4 fusion.65
  32.7 1.9 %collective-permute-start.3 = (bf16[1,2,4,4,64,128]{5,4,3,2,1,0:T(8,128)(2,1)}, bf16[1,2,4,4,64,128]{5,4,3,2,1,0:T(8,128)(2,1)}, u32[]{:S(2)}, u32[]{:S(2)}) collective-permute-start(bf16[1,2,4,4,64,128]{5,4,3,2,1,0:T(8,128)(2,1)} %fusion.65), channel_id=1, source_target_pairs={{508,0},{0,4},{4,8},{8,12},{12,16},{16,20},{20,24},{24,28},{28,32}... | collective-permute-start | bytes 1572872 | tf_op jit(solution)/shard_map/ppermute | solution.py:14
  34.6 0.8 fusion.177
  35.5 1.9 %collective-permute-start = (bf16[1,1,4,4,64,128]{5,4,3,2,1,0:T(8,128)(2,1)}, bf16[1,1,4,4,64,128]{5,4,3,2,1,0:T(8,128)(2,1)}, u32[]{:S(2)}, u32[]{:S(2)}) collective-permute-start(bf16[1,1,4,4,64,128]{5,4,3,2,1,0:T(8,128)(2,1)} %get-tuple-element.18), channel_id=1, source_target_pairs={{1,0},{2,1},{3,2},{0,3},{5,4},{6,5},{7,6},{4,7},{9,8},{10,9},{11,1... | collective-permute-start | bytes 786440 | tf_op jit(solution)/shard_map/ppermute | solution.py:14
  38.6 0.7 copy-done.4
  40.2 0.8 copy-done.5
  41.0 1.3 eq.15
  42.4 4.5 %collective-permute-done.1 = bf16[1,2,4,4,64,128]{5,4,3,2,1,0:T(8,128)(2,1)} collective-permute-done((bf16[1,2,4,4,64,128]{5,4,3,2,1,0:T(8,128)(2,1)}, bf16[1,2,4,4,64,128]{5,4,3,2,1,0:T(8,128)(2,1)}, u32[]{:S(2)}, u32[]{:S(2)}) %collective-permute-start.1) | collective-permute-done | bytes 524320 | tf_op jit(solution)/shard_map/ppermute | solution.py:14
  46.9 1.4 fusion.13
  48.3 5.4 %collective-permute-done = bf16[1,1,4,4,64,128]{5,4,3,2,1,0:T(8,128)(2,1)} collective-permute-done((bf16[1,1,4,4,64,128]{5,4,3,2,1,0:T(8,128)(2,1)}, bf16[1,1,4,4,64,128]{5,4,3,2,1,0:T(8,128)(2,1)}, u32[]{:S(2)}, u32[]{:S(2)}) %collective-permute-start) | collective-permute-done | bytes 262176 | tf_op jit(solution)/shard_map/ppermute | solution.py:14
  53.8 12.4 %collective-permute-done.3 = bf16[1,2,4,4,64,128]{5,4,3,2,1,0:T(8,128)(2,1)} collective-permute-done((bf16[1,2,4,4,64,128]{5,4,3,2,1,0:T(8,128)(2,1)}, bf16[1,2,4,4,64,128]{5,4,3,2,1,0:T(8,128)(2,1)}, u32[]{:S(2)}, u32[]{:S(2)}) %collective-permute-start.3) | collective-permute-done | bytes 524320 | tf_op jit(solution)/shard_map/ppermute | solution.py:14
  66.3 1.9 %fusion.178 = (bf16[1,2,4,4,64,128]{5,4,3,2,1,0:T(8,128)(2,1)S(1)}, f32[1,2,4,4,64,128]{5,4,3,2,1,0:T(8,128)S(1)}) fusion(bf16[1,2,4,4,64,128]{5,4,3,2,1,0:T(8,128)(2,1)} %collective-permute-done.3, bf16[1,1,4,4,64,128]{5,4,3,2,1,0:T(8,128)(2,1)S(1)} %copy-done.8, bf16[1,1,4,4,64,128]{5,4,3,2,1,0:T(8,128)(2,1)} %collective-permute-done.2, ...), kind=kOutput, calls=%fused_computation.227 | convolution fusion | flops 39583744 | bytes 7344128 | tf_op jit(solution)/shard_map/tzxyab,tzxybr->tzxyar/dot_general | solution.py:18
  68.2 1.9 %collective-permute-start.5 = (bf16[1,2,4,4,64,128]{5,4,3,2,1,0:T(8,128)(2,1)S(1)}, bf16[1,2,4,4,64,128]{5,4,3,2,1,0:T(8,128)(2,1)S(1)}, u32[]{:S(2)}, u32[]{:S(2)}) collective-permute-start(bf16[1,2,4,4,64,128]{5,4,3,2,1,0:T(8,128)(2,1)S(1)} %get-tuple-element.19), channel_id=1, source_target_pairs={{4,0},{8,4},{12,8},{16,12},{20,16},{24,20},{28,24},{32,28},{36,32}... | collective-permute-start | bytes 1572872 | tf_op jit(solution)/shard_map/ppermute | solution.py:14
  71.7 2.1 %collective-permute-start.6 = (bf16[1,1,4,4,64,128]{5,4,3,2,1,0:T(8,128)(2,1)S(1)}, bf16[1,1,4,4,64,128]{5,4,3,2,1,0:T(8,128)(2,1)S(1)}, u32[]{:S(2)}, u32[]{:S(2)}) collective-permute-start(bf16[1,1,4,4,64,128]{5,4,3,2,1,0:T(8,128)(2,1)S(1)} %get-tuple-element.11), channel_id=1, source_target_pairs={{3,0},{0,1},{1,2},{2,3},{7,4},{4,5},{5,6},{6,7},{11,8},{8,9},{9,10... | collective-permute-start | bytes 786440 | tf_op jit(solution)/shard_map/ppermute | solution.py:14
  73.8 3.6 %collective-permute-start.7 = (bf16[1,2,4,4,64,128]{5,4,3,2,1,0:T(8,128)(2,1)S(1)}, bf16[1,2,4,4,64,128]{5,4,3,2,1,0:T(8,128)(2,1)S(1)}, u32[]{:S(2)}, u32[]{:S(2)}) collective-permute-start(bf16[1,2,4,4,64,128]{5,4,3,2,1,0:T(8,128)(2,1)S(1)} %fusion.61), channel_id=1, source_target_pairs={{508,0},{0,4},{4,8},{8,12},{12,16},{16,20},{20,24},{24,28},{28,32}... | collective-permute-start | bytes 1572872 | tf_op jit(solution)/shard_map/ppermute | solution.py:14
  77.4 2.8 %collective-permute-start.4 = (bf16[1,1,4,4,64,128]{5,4,3,2,1,0:T(8,128)(2,1)S(1)}, bf16[1,1,4,4,64,128]{5,4,3,2,1,0:T(8,128)(2,1)S(1)}, u32[]{:S(2)}, u32[]{:S(2)}) collective-permute-start(bf16[1,1,4,4,64,128]{5,4,3,2,1,0:T(8,128)(2,1)S(1)} %get-tuple-element.14), channel_id=1, source_target_pairs={{1,0},{2,1},{3,2},{0,3},{5,4},{6,5},{7,6},{4,7},{9,8},{10,9},{11,1... | collective-permute-start | bytes 786440 | tf_op jit(solution)/shard_map/ppermute | solution.py:14
  82.0 10.6 %collective-permute-done.5 = bf16[1,2,4,4,64,128]{5,4,3,2,1,0:T(8,128)(2,1)S(1)} collective-permute-done((bf16[1,2,4,4,64,128]{5,4,3,2,1,0:T(8,128)(2,1)S(1)}, bf16[1,2,4,4,64,128]{5,4,3,2,1,0:T(8,128)(2,1)S(1)}, u32[]{:S(2)}, u32[]{:S(2)}) %collective-permute-start.5) | collective-permute-done | bytes 524320 | tf_op jit(solution)/shard_map/ppermute | solution.py:14
  93.0 10.2 %collective-permute-done.7 = bf16[1,2,4,4,64,128]{5,4,3,2,1,0:T(8,128)(2,1)S(1)} collective-permute-done((bf16[1,2,4,4,64,128]{5,4,3,2,1,0:T(8,128)(2,1)S(1)}, bf16[1,2,4,4,64,128]{5,4,3,2,1,0:T(8,128)(2,1)S(1)}, u32[]{:S(2)}, u32[]{:S(2)}) %collective-permute-start.7) | collective-permute-done | bytes 524320 | tf_op jit(solution)/shard_map/ppermute | solution.py:14
  104.0 1.9 %collective-permute-start.9 = (bf16[1,2,4,4,64,128]{5,4,3,2,1,0:T(8,128)(2,1)S(1)}, bf16[1,2,4,4,64,128]{5,4,3,2,1,0:T(8,128)(2,1)S(1)}, u32[]{:S(2)}, u32[]{:S(2)}) collective-permute-start(bf16[1,2,4,4,64,128]{5,4,3,2,1,0:T(8,128)(2,1)S(1)} %get-tuple-element.21), channel_id=1, source_target_pairs={{4,0},{8,4},{12,8},{16,12},{20,16},{24,20},{28,24},{32,28},{36,32}... | collective-permute-start | bytes 1572872 | tf_op jit(solution)/shard_map/ppermute | solution.py:14
  107.4 7.5 %collective-permute-start.10 = (bf16[1,1,4,4,64,128]{5,4,3,2,1,0:T(8,128)(2,1)S(1)}, bf16[1,1,4,4,64,128]{5,4,3,2,1,0:T(8,128)(2,1)S(1)}, u32[]{:S(2)}, u32[]{:S(2)}) collective-permute-start(bf16[1,1,4,4,64,128]{5,4,3,2,1,0:T(8,128)(2,1)S(1)} %get-tuple-element.7), channel_id=1, source_target_pairs={{3,0},{0,1},{1,2},{2,3},{7,4},{4,5},{5,6},{6,7},{11,8},{8,9},{9,10... | collective-permute-start | bytes 786440 | tf_op jit(solution)/shard_map/ppermute | solution.py:14
  114.9 3.6 %collective-permute-start.11 = (bf16[1,2,4,4,64,128]{5,4,3,2,1,0:T(8,128)(2,1)S(1)}, bf16[1,2,4,4,64,128]{5,4,3,2,1,0:T(8,128)(2,1)S(1)}, u32[]{:S(2)}, u32[]{:S(2)}) collective-permute-start(bf16[1,2,4,4,64,128]{5,4,3,2,1,0:T(8,128)(2,1)S(1)} %fusion.57), channel_id=1, source_target_pairs={{508,0},{0,4},{4,8},{8,12},{12,16},{16,20},{20,24},{24,28},{28,32}... | collective-permute-start | bytes 1572872 | tf_op jit(solution)/shard_map/ppermute | solution.py:14
  118.5 2.1 %collective-permute-start.8 = (bf16[1,1,4,4,64,128]{5,4,3,2,1,0:T(8,128)(2,1)S(1)}, bf16[1,1,4,4,64,128]{5,4,3,2,1,0:T(8,128)(2,1)S(1)}, u32[]{:S(2)}, u32[]{:S(2)}) collective-permute-start(bf16[1,1,4,4,64,128]{5,4,3,2,1,0:T(8,128)(2,1)S(1)} %get-tuple-element.10), channel_id=1, source_target_pairs={{1,0},{2,1},{3,2},{0,3},{5,4},{6,5},{7,6},{4,7},{9,8},{10,9},{11,1... | collective-permute-start | bytes 786440 | tf_op jit(solution)/shard_map/ppermute | solution.py:14
  122.8 13.7 %collective-permute-done.8 = bf16[1,1,4,4,64,128]{5,4,3,2,1,0:T(8,128)(2,1)S(1)} collective-permute-done((bf16[1,1,4,4,64,128]{5,4,3,2,1,0:T(8,128)(2,1)S(1)}, bf16[1,1,4,4,64,128]{5,4,3,2,1,0:T(8,128)(2,1)S(1)}, u32[]{:S(2)}, u32[]{:S(2)}) %collective-permute-start.8) | collective-permute-done | bytes 262176 | tf_op jit(solution)/shard_map/ppermute | solution.py:14
  136.5 10.0 %collective-permute-done.11 = bf16[1,2,4,4,64,128]{5,4,3,2,1,0:T(8,128)(2,1)S(1)} collective-permute-done((bf16[1,2,4,4,64,128]{5,4,3,2,1,0:T(8,128)(2,1)S(1)}, bf16[1,2,4,4,64,128]{5,4,3,2,1,0:T(8,128)(2,1)S(1)}, u32[]{:S(2)}, u32[]{:S(2)}) %collective-permute-start.11) | collective-permute-done | bytes 524320 | tf_op jit(solution)/shard_map/ppermute | solution.py:14
  146.6 0.7 fusion.44
  148.3 1.9 %fusion.69 = f32[16,8192]{1,0:T(8,128)} fusion(f32[4,8,64,128]{3,2,1,0:T(8,128)S(1)} %bitcast.321, s32[32]{0:T(128)S(1)} %copy-done.13), kind=kOutput, calls=%fused_computation.101 | convolution fusion | flops 50332160 | bytes 1572992 | tf_op jit(solution)/shard_map/dot_general | solution.py:75
  150.2 27.6 %all-gather.3.cloned.1.call-done = f32[64,8192]{1,0:T(8,128)} async-done(((f32[16,8192]{1,0:T(8,128)}), f32[64,8192]{1,0:T(8,128)}) %all-gather.3.cloned.1.call-update) | async-done | bytes 2097168 | tf_op jit(solution)/shard_map/all_gather | solution.py:76
  177.8 1.8 reduce_sum.9
  (96 shorter events, 12.5 us)
Async XLA Ops:
  7.2 30.3 %copy-start = (bf16[1,2,4,4,64,64]{5,4,3,2,1,0:T(8,128)(2,1)S(1)}, bf16[1,2,4,4,64,64]{5,4,3,2,1,0:T(8,128)(2,1)}, u32[]{:S(2)}) copy-start(bf16[1,2,4,4,64,64]{5,4,3,2,1,0:T(8,128)(2,1)} %param.7) | copy-start | bytes 786436
  7.2 24.1 %copy-start.2 = (bf16[1,2,4,4,64,128]{5,4,3,2,1,0:T(8,128)(2,1)S(1)}, bf16[1,2,4,4,64,128]{5,4,3,2,1,0:T(8,128)(2,1)}, u32[]{:S(2)}) copy-start(bf16[1,2,4,4,64,128]{5,4,3,2,1,0:T(8,128)(2,1)} %param.6) | copy-start | bytes 1572868
  7.2 24.1 %copy-start.1 = (bf16[1,2,4,4,64,256]{5,4,3,2,1,0:T(8,128)(2,1)S(1)}, bf16[1,2,4,4,64,256]{5,4,3,2,1,0:T(8,128)(2,1)}, u32[]{:S(2)}) copy-start(bf16[1,2,4,4,64,256]{5,4,3,2,1,0:T(8,128)(2,1)} %param.8) | copy-start | bytes 3145732
  7.2 170.6 %all-gather.3.cloned.1.call-start = ((), (), s32[]{:S(2)}) async-start(), calls=%async_computation | async-start | bytes 2621440 | tf_op jit(solution)/shard_map/all_gather | solution.py:76
  7.2 39.7 %collective-permute-start.1 = (bf16[1,2,4,4,64,128]{5,4,3,2,1,0:T(8,128)(2,1)}, bf16[1,2,4,4,64,128]{5,4,3,2,1,0:T(8,128)(2,1)}, u32[]{:S(2)}, u32[]{:S(2)}) collective-permute-start(bf16[1,2,4,4,64,128]{5,4,3,2,1,0:T(8,128)(2,1)} %param.6), channel_id=1, source_target_pairs={{4,0},{8,4},{12,8},{16,12},{20,16},{24,20},{28,24},{32,28},{36,32}... | collective-permute-start | bytes 1572872 | tf_op jit(solution)/shard_map/ppermute | solution.py:14
  25.7 11.8 %copy-start.11 = (f32[2,4,4]{2,1,0:T(4,128)}, f32[2,4,4]{2,1,0:T(4,128)S(1)}, u32[]{:S(2)}) copy-start(f32[2,4,4]{2,1,0:T(4,128)S(1)} %get-tuple-element.6) | copy-start | bytes 388
  28.1 20.2 %collective-permute-start.2 = (bf16[1,1,4,4,64,128]{5,4,3,2,1,0:T(8,128)(2,1)}, bf16[1,1,4,4,64,128]{5,4,3,2,1,0:T(8,128)(2,1)}, u32[]{:S(2)}, u32[]{:S(2)}) collective-permute-start(bf16[1,1,4,4,64,128]{5,4,3,2,1,0:T(8,128)(2,1)} %get-tuple-element.15), channel_id=1, source_target_pairs={{3,0},{0,1},{1,2},{2,3},{7,4},{4,5},{5,6},{6,7},{11,8},{8,9},{9,10... | collective-permute-start | bytes 786440 | tf_op jit(solution)/shard_map/ppermute | solution.py:14
  32.7 33.5 %collective-permute-start.3 = (bf16[1,2,4,4,64,128]{5,4,3,2,1,0:T(8,128)(2,1)}, bf16[1,2,4,4,64,128]{5,4,3,2,1,0:T(8,128)(2,1)}, u32[]{:S(2)}, u32[]{:S(2)}) collective-permute-start(bf16[1,2,4,4,64,128]{5,4,3,2,1,0:T(8,128)(2,1)} %fusion.65), channel_id=1, source_target_pairs={{508,0},{0,4},{4,8},{8,12},{12,16},{16,20},{20,24},{24,28},{28,32}... | collective-permute-start | bytes 1572872 | tf_op jit(solution)/shard_map/ppermute | solution.py:14
  35.5 18.3 %collective-permute-start = (bf16[1,1,4,4,64,128]{5,4,3,2,1,0:T(8,128)(2,1)}, bf16[1,1,4,4,64,128]{5,4,3,2,1,0:T(8,128)(2,1)}, u32[]{:S(2)}, u32[]{:S(2)}) collective-permute-start(bf16[1,1,4,4,64,128]{5,4,3,2,1,0:T(8,128)(2,1)} %get-tuple-element.18), channel_id=1, source_target_pairs={{1,0},{2,1},{3,2},{0,3},{5,4},{6,5},{7,6},{4,7},{9,8},{10,9},{11,1... | collective-permute-start | bytes 786440 | tf_op jit(solution)/shard_map/ppermute | solution.py:14
  39.6 26.6 %slice-start.2 = ((bf16[1,2,4,4,64,128]{5,4,3,2,1,0:T(8,128)(2,1)}), bf16[1,2,3,4,64,128]{5,4,3,2,1,0:T(8,128)(2,1)S(1)}, s32[]{:S(2)}) async-start(bf16[1,2,4,4,64,128]{5,4,3,2,1,0:T(8,128)(2,1)} %copy-done.4), calls=%async_computation.3 | async-start | bytes 786432 | tf_op jit(solution)/shard_map/jit(_roll_static)/slice | solution.py:53
  42.4 23.9 %slice-start.3 = ((bf16[1,2,4,4,64,128]{5,4,3,2,1,0:T(8,128)(2,1)}), bf16[1,2,1,4,64,128]{5,4,3,2,1,0:T(8,128)(2,1)S(1)}, s32[]{:S(2)}) async-start(bf16[1,2,4,4,64,128]{5,4,3,2,1,0:T(8,128)(2,1)} %copy-done.4), calls=%async_computation.4 | async-start | bytes 262144 | tf_op jit(solution)/shard_map/jit(_roll_static)/slice | solution.py:53
  42.4 23.9 %slice-start.4 = ((bf16[1,2,4,4,64,128]{5,4,3,2,1,0:T(8,128)(2,1)}), bf16[1,2,4,3,64,128]{5,4,3,2,1,0:T(8,128)(2,1)S(1)}, s32[]{:S(2)}) async-start(bf16[1,2,4,4,64,128]{5,4,3,2,1,0:T(8,128)(2,1)} %copy-done.5), calls=%async_computation.5 | async-start | bytes 786432 | tf_op jit(solution)/shard_map/jit(_roll_static)/slice | solution.py:53
  42.4 23.9 %slice-start.5 = ((bf16[1,2,4,4,64,128]{5,4,3,2,1,0:T(8,128)(2,1)}), bf16[1,2,4,1,64,128]{5,4,3,2,1,0:T(8,128)(2,1)S(1)}, s32[]{:S(2)}) async-start(bf16[1,2,4,4,64,128]{5,4,3,2,1,0:T(8,128)(2,1)} %copy-done.5), calls=%async_computation.6 | async-start | bytes 262144 | tf_op jit(solution)/shard_map/jit(_roll_static)/slice | solution.py:53
  42.4 23.9 %copy-start.8 = (bf16[1,1,4,4,64,128]{5,4,3,2,1,0:T(8,128)(2,1)S(1)}, bf16[1,1,4,4,64,128]{5,4,3,2,1,0:T(8,128)(2,1)}, u32[]{:S(2)}) copy-start(bf16[1,1,4,4,64,128]{5,4,3,2,1,0:T(8,128)(2,1)} %get-tuple-element.16) | copy-start | bytes 786436
  42.4 23.9 %copy-start.9 = (bf16[1,1,4,4,64,128]{5,4,3,2,1,0:T(8,128)(2,1)S(1)}, bf16[1,1,4,4,64,128]{5,4,3,2,1,0:T(8,128)(2,1)}, u32[]{:S(2)}) copy-start(bf16[1,1,4,4,64,128]{5,4,3,2,1,0:T(8,128)(2,1)} %get-tuple-element.17) | copy-start | bytes 786436
  68.2 24.3 %collective-permute-start.5 = (bf16[1,2,4,4,64,128]{5,4,3,2,1,0:T(8,128)(2,1)S(1)}, bf16[1,2,4,4,64,128]{5,4,3,2,1,0:T(8,128)(2,1)S(1)}, u32[]{:S(2)}, u32[]{:S(2)}) collective-permute-start(bf16[1,2,4,4,64,128]{5,4,3,2,1,0:T(8,128)(2,1)S(1)} %get-tuple-element.19), channel_id=1, source_target_pairs={{4,0},{8,4},{12,8},{16,12},{20,16},{24,20},{28,24},{32,28},{36,32}... | collective-permute-start | bytes 1572872 | tf_op jit(solution)/shard_map/ppermute | solution.py:14
  71.5 9.0 %copy-start.6 = (bf16[1,2,4,4,64,128]{5,4,3,2,1,0:T(8,128)(2,1)}, bf16[1,2,4,4,64,128]{5,4,3,2,1,0:T(8,128)(2,1)S(1)}, u32[]{:S(2)}) copy-start(bf16[1,2,4,4,64,128]{5,4,3,2,1,0:T(8,128)(2,1)S(1)} %fusion.64) | copy-start | bytes 1572868
  71.6 9.0 %copy-start.12 = (f32[2,4,4]{2,1,0:T(4,128)S(1)}, f32[2,4,4]{2,1,0:T(4,128)}, u32[]{:S(2)}) copy-start(f32[2,4,4]{2,1,0:T(4,128)} %copy-done.11) | copy-start | bytes 388
  71.7 21.3 %collective-permute-start.6 = (bf16[1,1,4,4,64,128]{5,4,3,2,1,0:T(8,128)(2,1)S(1)}, bf16[1,1,4,4,64,128]{5,4,3,2,1,0:T(8,128)(2,1)S(1)}, u32[]{:S(2)}, u32[]{:S(2)}) collective-permute-start(bf16[1,1,4,4,64,128]{5,4,3,2,1,0:T(8,128)(2,1)S(1)} %get-tuple-element.11), channel_id=1, source_target_pairs={{3,0},{0,1},{1,2},{2,3},{7,4},{4,5},{5,6},{6,7},{11,8},{8,9},{9,10... | collective-permute-start | bytes 786440 | tf_op jit(solution)/shard_map/ppermute | solution.py:14
  73.8 29.4 %collective-permute-start.7 = (bf16[1,2,4,4,64,128]{5,4,3,2,1,0:T(8,128)(2,1)S(1)}, bf16[1,2,4,4,64,128]{5,4,3,2,1,0:T(8,128)(2,1)S(1)}, u32[]{:S(2)}, u32[]{:S(2)}) collective-permute-start(bf16[1,2,4,4,64,128]{5,4,3,2,1,0:T(8,128)(2,1)S(1)} %fusion.61), channel_id=1, source_target_pairs={{508,0},{0,4},{4,8},{8,12},{12,16},{16,20},{20,24},{24,28},{28,32}... | collective-permute-start | bytes 1572872 | tf_op jit(solution)/shard_map/ppermute | solution.py:14
  77.4 15.5 %collective-permute-start.4 = (bf16[1,1,4,4,64,128]{5,4,3,2,1,0:T(8,128)(2,1)S(1)}, bf16[1,1,4,4,64,128]{5,4,3,2,1,0:T(8,128)(2,1)S(1)}, u32[]{:S(2)}, u32[]{:S(2)}) collective-permute-start(bf16[1,1,4,4,64,128]{5,4,3,2,1,0:T(8,128)(2,1)S(1)} %get-tuple-element.14), channel_id=1, source_target_pairs={{1,0},{2,1},{3,2},{0,3},{5,4},{6,5},{7,6},{4,7},{9,8},{10,9},{11,1... | collective-permute-start | bytes 786440 | tf_op jit(solution)/shard_map/ppermute | solution.py:14
  81.3 21.9 %slice-start.6 = ((bf16[1,2,4,4,64,128]{5,4,3,2,1,0:T(8,128)(2,1)}), bf16[1,2,3,4,64,128]{5,4,3,2,1,0:T(8,128)(2,1)S(1)}, s32[]{:S(2)}) async-start(bf16[1,2,4,4,64,128]{5,4,3,2,1,0:T(8,128)(2,1)} %copy-done.6), calls=%async_computation.7 | async-start | bytes 786432 | tf_op jit(solution)/shard_map/jit(_roll_static)/slice | solution.py:53
  81.3 21.9 %slice-start.7 = ((bf16[1,2,4,4,64,128]{5,4,3,2,1,0:T(8,128)(2,1)}), bf16[1,2,1,4,64,128]{5,4,3,2,1,0:T(8,128)(2,1)S(1)}, s32[]{:S(2)}) async-start(bf16[1,2,4,4,64,128]{5,4,3,2,1,0:T(8,128)(2,1)} %copy-done.6), calls=%async_computation.8 | async-start | bytes 262144 | tf_op jit(solution)/shard_map/jit(_roll_static)/slice | solution.py:53
  104.0 18.5 %collective-permute-start.9 = (bf16[1,2,4,4,64,128]{5,4,3,2,1,0:T(8,128)(2,1)S(1)}, bf16[1,2,4,4,64,128]{5,4,3,2,1,0:T(8,128)(2,1)S(1)}, u32[]{:S(2)}, u32[]{:S(2)}) collective-permute-start(bf16[1,2,4,4,64,128]{5,4,3,2,1,0:T(8,128)(2,1)S(1)} %get-tuple-element.21), channel_id=1, source_target_pairs={{4,0},{8,4},{12,8},{16,12},{20,16},{24,20},{28,24},{32,28},{36,32}... | collective-permute-start | bytes 1572872 | tf_op jit(solution)/shard_map/ppermute | solution.py:14
  107.3 13.7 %copy-start.3 = (bf16[1,2,4,4,64,128]{5,4,3,2,1,0:T(8,128)(2,1)}, bf16[1,2,4,4,64,128]{5,4,3,2,1,0:T(8,128)(2,1)S(1)}, u32[]{:S(2)}) copy-start(bf16[1,2,4,4,64,128]{5,4,3,2,1,0:T(8,128)(2,1)S(1)} %fusion.60) | copy-start | bytes 1572868
  107.4 15.5 %collective-permute-start.10 = (bf16[1,1,4,4,64,128]{5,4,3,2,1,0:T(8,128)(2,1)S(1)}, bf16[1,1,4,4,64,128]{5,4,3,2,1,0:T(8,128)(2,1)S(1)}, u32[]{:S(2)}, u32[]{:S(2)}) collective-permute-start(bf16[1,1,4,4,64,128]{5,4,3,2,1,0:T(8,128)(2,1)S(1)} %get-tuple-element.7), channel_id=1, source_target_pairs={{3,0},{0,1},{1,2},{2,3},{7,4},{4,5},{5,6},{6,7},{11,8},{8,9},{9,10... | collective-permute-start | bytes 786440 | tf_op jit(solution)/shard_map/ppermute | solution.py:14
  114.9 31.7 %collective-permute-start.11 = (bf16[1,2,4,4,64,128]{5,4,3,2,1,0:T(8,128)(2,1)S(1)}, bf16[1,2,4,4,64,128]{5,4,3,2,1,0:T(8,128)(2,1)S(1)}, u32[]{:S(2)}, u32[]{:S(2)}) collective-permute-start(bf16[1,2,4,4,64,128]{5,4,3,2,1,0:T(8,128)(2,1)S(1)} %fusion.57), channel_id=1, source_target_pairs={{508,0},{0,4},{4,8},{8,12},{12,16},{16,20},{20,24},{24,28},{28,32}... | collective-permute-start | bytes 1572872 | tf_op jit(solution)/shard_map/ppermute | solution.py:14
  118.5 18.0 %collective-permute-start.8 = (bf16[1,1,4,4,64,128]{5,4,3,2,1,0:T(8,128)(2,1)S(1)}, bf16[1,1,4,4,64,128]{5,4,3,2,1,0:T(8,128)(2,1)S(1)}, u32[]{:S(2)}, u32[]{:S(2)}) collective-permute-start(bf16[1,1,4,4,64,128]{5,4,3,2,1,0:T(8,128)(2,1)S(1)} %get-tuple-element.10), channel_id=1, source_target_pairs={{1,0},{2,1},{3,2},{0,3},{5,4},{6,5},{7,6},{4,7},{9,8},{10,9},{11,1... | collective-permute-start | bytes 786440 | tf_op jit(solution)/shard_map/ppermute | solution.py:14
  121.7 24.8 %slice-start = ((bf16[1,2,4,4,64,128]{5,4,3,2,1,0:T(8,128)(2,1)}), bf16[1,2,3,4,64,128]{5,4,3,2,1,0:T(8,128)(2,1)S(1)}, s32[]{:S(2)}) async-start(bf16[1,2,4,4,64,128]{5,4,3,2,1,0:T(8,128)(2,1)} %copy-done.3), calls=%async_computation.1 | async-start | bytes 786432 | tf_op jit(solution)/shard_map/jit(_roll_static)/slice | solution.py:53
  121.8 24.8 %slice-start.1 = ((bf16[1,2,4,4,64,128]{5,4,3,2,1,0:T(8,128)(2,1)}), bf16[1,2,1,4,64,128]{5,4,3,2,1,0:T(8,128)(2,1)S(1)}, s32[]{:S(2)}) async-start(bf16[1,2,4,4,64,128]{5,4,3,2,1,0:T(8,128)(2,1)} %copy-done.3), calls=%async_computation.2 | async-start | bytes 262144 | tf_op jit(solution)/shard_map/jit(_roll_static)/slice | solution.py:53
  146.6 1.0 copy-start.10
  147.6 2.6 %copy-start.7 = (bf16[1,2,4,4,64,128]{5,4,3,2,1,0:T(8,128)(2,1)}, bf16[1,2,4,4,64,128]{5,4,3,2,1,0:T(8,128)(2,1)S(1)}, u32[]{:S(2)}) copy-start(bf16[1,2,4,4,64,128]{5,4,3,2,1,0:T(8,128)(2,1)S(1)} %fusion.44) | copy-start | bytes 1572868
  (3 other events, 2.2 us)
Sparse Core Ops, SparseCore 0:
  150.3 27.4 all-gather.2
